TPU v7x, 32 devices: a whole 2x2x4 slice. The times are simulated.
32 devices in a mesh: ep: 8 (over z, y), tp: 4 (over x, core).
Axes of the slice: x: 2, y: 2, z: 4, core: 2. Of those that a mesh axis runs over, the one named last changes fastest.
Arguments:
- tokens: bfloat16 [4096, 1536], P(('ep', 'tp')), may hold values from -6 to 6
- norm_gain: float32 [1536], replicated, may hold values from 0.5 to 1.5
- query_matrix: bfloat16 [1536, 1536], P(None, 'tp'), may hold values from -0.15625 to 0.15625
- key_matrix: bfloat16 [1536, 512], P(None, 'tp'), may hold values from -0.15625 to 0.15625
- value_matrix: bfloat16 [1536, 512], P(None, 'tp'), may hold values from -0.15625 to 0.15625
- out_weight: bfloat16 [1536, 1536], P('tp'), may hold values from -1.25 to 1.25
- moe_gain: float32 [1536], replicated, may hold values from 0.5 to 1.5
- router_weight: bfloat16 [1536, 40], replicated, may hold values from -0.0390625 to 0.0390625
- gate_weight: bfloat16 [40, 1536, 512], P('ep', None, 'tp'), may hold values from -0.15625 to 0.15625
- up_weight: bfloat16 [40, 1536, 512], P('ep', None, 'tp'), may hold values from -0.15625 to 0.15625
- down_weight: bfloat16 [40, 512, 1536], P('ep', 'tp'), may hold values from -2 to 2
- cotangent: bfloat16 [4096, 1536], P(('ep', 'tp')), may hold values from -6 to 6
- expert_ids: int32 [4096, 8], P(('ep', 'tp')), may hold values from 0 to 39, all different within a row; in each aligned block of 128 rows (0 to 127, 128 to 255, ...) at most 32 rows name the same one
- segments: int32 [8, 512], P('ep'), may hold values from 0 to 3, never falling along the last dimension, each value on 1 to 256 neighbouring positions
- valid_mask: int32 [8, 512], P('ep'), may hold values from 0 to 1, as said below
Outputs:
- output: bfloat16 [4096, 1536], P(('ep', 'tp'))
- input_grad: float32 [4096, 1536], P(('ep', 'tp'))
- norm_gain_grad: float32 [1536], replicated
- query_grad: float32 [1536, 1536], P(None, 'tp')
- key_grad: float32 [1536, 512], P(None, 'tp')
- value_grad: float32 [1536, 512], P(None, 'tp')
- out_grad: float32 [1536, 1536], P('tp')
- moe_gain_grad: float32 [1536], replicated
- router_grad: float32 [1536, 40], replicated
- gate_grad: float32 [40, 1536, 512], P('ep', None, 'tp')
- up_grad: float32 [40, 1536, 512], P('ep', None, 'tp')
- down_grad: float32 [40, 512, 1536], P('ep', 'tp')
Inputs may be any that keep to these rules, and one draw needn't show every extreme that they name: `expert_ids`: each row names 8 different experts. Among the 128 rows of one device (aligned blocks of 128 rows) no expert is named by more than 32 rows, a bound that some block reaches. `segments`: document numbers never fall along a sequence; each document has 1 to 256 tokens, one exactly 256. `valid_mask`: in each sequence the ones form a prefix of 384 tokens or more; the first sequence has no padding.
All inputs are finite; a program needn't handle non-finite values.
Results may differ from a plain program's by a relative error of at most 0.015.
Values may be sent and summed in bfloat16 or wider, within the bound.
No kernel may reach another device: no remote copies, remote signals or barrier semaphores. Data moves between devices by JAX's collectives and lax.ppermute only.
A program may use at most 320 MiB of HBM per device.

v0:
```python
import math
import jax
import jax.numpy as jnp
from jax import lax
from jax.sharding import PartitionSpec as P

HEAD_SIZE_DIM = 64
EPS = 1e-06
HIGH_PRECISION = lax.Precision.HIGHEST


def rms_norm(activation, gain_vec):
    factor = lax.rsqrt(jnp.mean(activation * activation, axis=-1, keepdims=True) + EPS)
    return activation * factor * gain_vec


def rotate(vectors, cos_table, sin_table):
    half_size = vectors.shape[-1] // 2
    first_half = vectors[..., :half_size]
    second_half = vectors[..., half_size:]
    return jnp.concatenate(
        [
            first_half * cos_table - second_half * sin_table,
            second_half * cos_table + first_half * sin_table,
        ],
        axis=-1,
    )


def angle_tables(span_length, head_size):
    half_size = head_size // 2
    inverse = jnp.exp(
        -math.log(10000.0) * jnp.arange(half_size, dtype=jnp.float32) * 2.0 / head_size
    )
    angles = jnp.arange(span_length, dtype=jnp.float32)[:, None] * inverse[None, :]
    return (jnp.cos(angles), jnp.sin(angles))


def swiglu(gate_val, up_val):
    return jax.nn.silu(gate_val) * up_val


def softmax_rows(logits):
    return jax.nn.softmax(logits, axis=-1)


def block_mask(segment_row, live_row, offset, height):
    span_length = segment_row.shape[0]
    key_places = jnp.arange(span_length)
    query_places = offset + jnp.arange(height)
    same_doc = segment_row[:, None] == segment_row[None, :]
    causal = key_places[None, :] <= query_places[:, None]
    usable = (live_row[None, :] > 0) | (key_places[None, :] == query_places[:, None])
    return same_doc & causal & usable


def block_scores(query_block, key_val, allowed, factor):
    scores = (
        jnp.einsum("qgrd,kgd->grqk", query_block, key_val, preferred_element_type=jnp.float32)
        * factor
    )
    return jnp.where(allowed[None, None], scores, -1e30)


def group_rows(boxes):
    return lax.all_gather(boxes, "tp", axis=0, tiled=True)


def dispatch_rows(boxes):
    return lax.all_to_all(boxes, "ep", split_axis=1, concat_axis=1, tiled=True)


def return_rows(boxes):
    return lax.all_to_all(boxes, "ep", split_axis=1, concat_axis=1, tiled=True)


def local(
    tokens,
    norm_gain,
    query_matrix,
    key_matrix,
    value_matrix,
    out_weight,
    moe_gain,
    router_weight,
    gate_weight,
    up_weight,
    down_weight,
    cotangent,
    expert_ids,
    segments,
    valid_mask,
):
    quarter = tokens.shape[0]
    width = tokens.shape[1]
    groups = lax.axis_size("tp")
    owners = lax.axis_size("ep")
    my_part = lax.axis_index("tp")
    seq_len = quarter * groups
    head_size = HEAD_SIZE_DIM
    kv_heads = key_matrix.shape[1] // head_size
    q_heads = query_matrix.shape[1] // head_size
    group_factor = q_heads // kv_heads
    local_experts = gate_weight.shape[0]
    experts_all = router_weight.shape[1]
    chosen_count = expert_ids.shape[1]
    slots = max(8, 3 * quarter * chosen_count // (2 * experts_all) // 8 * 8)
    factor = 1.0 / math.sqrt(head_size)
    segment_row = segments[0]
    live_row = valid_mask[0]
    x_float = tokens.astype(jnp.float32)
    normed = rms_norm(x_float, norm_gain).astype(jnp.bfloat16)
    normed_all = lax.all_gather(normed, "tp", axis=0, tiled=True)
    query_unrotated = jnp.dot(normed_all, query_matrix, preferred_element_type=jnp.float32).reshape(
        seq_len, kv_heads, group_factor, head_size
    )
    key_unrotated = jnp.dot(normed_all, key_matrix, preferred_element_type=jnp.float32).reshape(
        seq_len, kv_heads, head_size
    )
    value_vectors = (
        jnp.dot(normed_all, value_matrix, preferred_element_type=jnp.float32)
        .astype(jnp.bfloat16)
        .reshape(seq_len, kv_heads, head_size)
    )
    cos_table, sin_table = angle_tables(seq_len, head_size)
    cos_query = cos_table[:, None, None, :]
    sin_query = sin_table[:, None, None, :]
    cos_key = cos_table[:, None, :]
    sin_key = sin_table[:, None, :]
    query_val = rotate(query_unrotated, cos_query, sin_query).astype(jnp.bfloat16)
    key_val = rotate(key_unrotated, cos_key, sin_key).astype(jnp.bfloat16)
    height = min(512, seq_len)
    offset = 0
    allowed = block_mask(segment_row, live_row, offset, height)
    scores = block_scores(query_val, key_val, allowed, factor)
    peak = jnp.max(scores, axis=-1, keepdims=True)
    expo = jnp.exp(scores - peak)
    denom = jnp.sum(expo, axis=-1, keepdims=True)
    weights = (expo / denom).astype(jnp.bfloat16)
    mixed = jnp.einsum("grqk,kgd->qgrd", weights, value_vectors, preferred_element_type=jnp.float32)
    outputs = mixed.reshape(height, q_heads * head_size)
    log_sums = [peak + jnp.log(denom)]
    attended = outputs.astype(jnp.bfloat16)
    branch = lax.psum_scatter(
        jnp.dot(attended, out_weight, preferred_element_type=jnp.float32),
        "tp",
        scatter_dimension=0,
        tiled=True,
    )
    middle = x_float + branch
    moe_in = rms_norm(middle, moe_gain).astype(jnp.bfloat16)
    logits = jnp.dot(moe_in, router_weight, preferred_element_type=jnp.float32)
    router = softmax_rows(logits)
    my_valid = lax.dynamic_slice_in_dim(live_row, my_part * quarter, quarter, 0)
    valid_float = my_valid.astype(jnp.float32)
    picked = jnp.take_along_axis(router, expert_ids, axis=1) * valid_float[:, None]
    flat_ids = expert_ids.reshape(-1)
    flat_live = jnp.repeat(my_valid, chosen_count)
    onehot = (flat_ids[:, None] == jnp.arange(experts_all)[None, :]).astype(jnp.int32) * flat_live[
        :, None
    ]
    earlier = jnp.cumsum(onehot, axis=0) - onehot
    slot_of = jnp.sum(earlier * onehot, axis=1)
    target = jnp.where(flat_live > 0, flat_ids, experts_all)
    safe_target = jnp.minimum(target, experts_all - 1)

    def pack(row_block):
        boxes = jnp.zeros((experts_all, slots, width), jnp.bfloat16)
        boxes = boxes.at[target, slot_of].set(row_block, mode="drop")
        return boxes.reshape(1, owners, local_experts * slots, width)

    def unpack(boxes):
        flat_boxes = boxes.reshape(experts_all, slots, width)
        taken = flat_boxes[safe_target, slot_of]
        taken = jnp.where(flat_live[:, None] > 0, taken, jnp.zeros_like(taken))
        return taken.reshape(quarter, chosen_count, width)

    sent = pack(jnp.repeat(moe_in, chosen_count, axis=0))
    full_gate, full_up, full_down = (gate_weight, up_weight, down_weight)
    arrived = dispatch_rows(group_rows(sent))
    expert_rows = arrived.reshape(groups, owners, local_experts, slots, width)
    gate_val = jnp.einsum(
        "tsecd,edf->tsecf", expert_rows, gate_weight, preferred_element_type=jnp.float32
    )
    up_val = jnp.einsum(
        "tsecd,edf->tsecf", expert_rows, up_weight, preferred_element_type=jnp.float32
    )
    hidden = swiglu(gate_val, up_val).astype(jnp.bfloat16)
    result = jnp.einsum("tsecf,efd->tsecd", hidden, down_weight, preferred_element_type=jnp.float32)
    finished = lax.psum_scatter(
        result.reshape(1 * lax.axis_size("tp"), owners, local_experts * slots, width).astype(
            jnp.bfloat16
        ),
        "tp",
        scatter_dimension=0,
        tiled=True,
    )
    returned = lax.dynamic_slice_in_dim(return_rows(group_rows(finished)), my_part, 1, 0)
    result_rows = unpack(returned).astype(jnp.float32)
    output = (middle + jnp.sum(picked[:, :, None] * result_rows, axis=1)).astype(jnp.bfloat16)
    grad_out = cotangent.astype(jnp.float32)
    grad_picked = jnp.einsum("tkd,td->tk", result_rows, grad_out, precision=HIGH_PRECISION)
    onehot_float = (expert_ids[:, :, None] == jnp.arange(experts_all)[None, None, :]).astype(
        jnp.float32
    )
    grad_router = jnp.sum(onehot_float * (grad_picked * valid_float[:, None])[:, :, None], axis=1)
    _, soft_back = jax.vjp(softmax_rows, logits)
    grad_logits = soft_back(grad_router)[0]
    grad_result = (
        (picked[:, :, None] * grad_out[:, None, :])
        .astype(jnp.bfloat16)
        .reshape(quarter * chosen_count, width)
    )
    grad_sent = pack(grad_result)
    grad_arrived = dispatch_rows(group_rows(grad_sent))
    grad_rows = grad_arrived.reshape(groups, owners, local_experts, slots, width)
    gate_all = jnp.einsum(
        "tsecd,edf->tsecf", expert_rows, full_gate, preferred_element_type=jnp.float32
    )
    up_all = jnp.einsum(
        "tsecd,edf->tsecf", expert_rows, full_up, preferred_element_type=jnp.float32
    )
    hidden_all, swiglu_back = jax.vjp(swiglu, gate_all, up_all)
    hidden_low = hidden_all.astype(jnp.bfloat16)
    grad_hidden = jnp.einsum(
        "tsecd,efd->tsecf", grad_rows, full_down, preferred_element_type=jnp.float32
    )
    grad_gate_f, grad_up_f = swiglu_back(grad_hidden)
    grad_gate_rows = grad_gate_f.astype(jnp.bfloat16)
    grad_up_rows = grad_up_f.astype(jnp.bfloat16)
    down_grad = jnp.einsum(
        "tsecf,tsecd->efd", hidden_low, grad_rows, preferred_element_type=jnp.float32
    )
    gate_grad = jnp.einsum(
        "tsecd,tsecf->edf", expert_rows, grad_gate_rows, preferred_element_type=jnp.float32
    )
    up_grad = jnp.einsum(
        "tsecd,tsecf->edf", expert_rows, grad_up_rows, preferred_element_type=jnp.float32
    )
    summed = jnp.einsum(
        "tsecf,edf->tsecd", grad_gate_rows, gate_weight, preferred_element_type=jnp.float32
    )
    summed = summed + jnp.einsum(
        "tsecf,edf->tsecd", grad_up_rows, up_weight, preferred_element_type=jnp.float32
    )
    grad_finished = lax.psum_scatter(
        summed.reshape(1 * lax.axis_size("tp"), owners, local_experts * slots, width).astype(
            jnp.bfloat16
        ),
        "tp",
        scatter_dimension=0,
        tiled=True,
    )
    grad_returned = lax.dynamic_slice_in_dim(return_rows(group_rows(grad_finished)), my_part, 1, 0)
    grad_copies = unpack(grad_returned).astype(jnp.float32)
    router_float = router_weight.astype(jnp.float32)
    grad_moe_in = jnp.sum(grad_copies, axis=1) + jnp.dot(
        grad_logits, router_float.T, precision=HIGH_PRECISION
    )
    router_grad = jnp.dot(moe_in.astype(jnp.float32).T, grad_logits, precision=HIGH_PRECISION)
    _, norm_two_back = jax.vjp(rms_norm, middle, moe_gain)
    grad_mid_norm, moe_gain_grad = norm_two_back(grad_moe_in)
    grad_middle = grad_out + grad_mid_norm
    grad_branch = lax.all_gather(grad_middle.astype(jnp.bfloat16), "tp", axis=0, tiled=True)
    out_grad = jnp.einsum("sh,sd->hd", attended, grad_branch, preferred_element_type=jnp.float32)
    grad_attended = jnp.einsum(
        "sd,hd->sh", grad_branch, out_weight, preferred_element_type=jnp.float32
    ).astype(jnp.bfloat16)
    grad_attended = grad_attended.reshape(seq_len, kv_heads, group_factor, head_size)
    query_parts = []
    key_total = jnp.zeros((seq_len, kv_heads, head_size), jnp.float32)
    value_total = jnp.zeros((seq_len, kv_heads, head_size), jnp.float32)
    for block_no, offset in enumerate(range(0, seq_len, height)):
        allowed = block_mask(segment_row, live_row, offset, height)
        scores = block_scores(query_val, key_val, allowed, factor)
        probs = jnp.where(allowed[None, None], jnp.exp(scores - log_sums[block_no]), 0.0)
        grad_probs = jnp.einsum(
            "qgrd,kgd->grqk", grad_attended, value_vectors, preferred_element_type=jnp.float32
        )
        centre = jnp.sum(probs * grad_probs, axis=-1, keepdims=True)
        grad_scores = (probs * (grad_probs - centre)).astype(jnp.bfloat16)
        query_parts.append(
            jnp.einsum("grqk,kgd->qgrd", grad_scores, key_val, preferred_element_type=jnp.float32)
            * factor
        )
        key_total = (
            jnp.einsum("grqk,qgrd->kgd", grad_scores, query_val, preferred_element_type=jnp.float32)
            * factor
        )
        value_total = jnp.einsum(
            "grqk,qgrd->kgd",
            probs.astype(jnp.bfloat16),
            grad_attended,
            preferred_element_type=jnp.float32,
        )
    grad_query_rot = query_parts[0]
    _, query_back = jax.vjp(lambda vectors: rotate(vectors, cos_query, sin_query), query_unrotated)
    _, key_back = jax.vjp(lambda vectors: rotate(vectors, cos_key, sin_key), key_unrotated)
    grad_q_pre = (
        query_back(grad_query_rot)[0].astype(jnp.bfloat16).reshape(seq_len, q_heads * head_size)
    )
    grad_k_pre = key_back(key_total)[0].astype(jnp.bfloat16).reshape(seq_len, kv_heads * head_size)
    grad_value = value_total.astype(jnp.bfloat16).reshape(seq_len, kv_heads * head_size)
    query_grad = jnp.einsum("sd,sh->dh", normed_all, grad_q_pre, preferred_element_type=jnp.float32)
    key_grad = jnp.einsum("sd,sh->dh", normed_all, grad_k_pre, preferred_element_type=jnp.float32)
    value_grad = jnp.einsum("sd,sh->dh", normed_all, grad_value, preferred_element_type=jnp.float32)
    summed = jnp.einsum("sh,dh->sd", grad_q_pre, query_matrix, preferred_element_type=jnp.float32)
    summed = summed + jnp.einsum(
        "sh,dh->sd", grad_k_pre, key_matrix, preferred_element_type=jnp.float32
    )
    summed = summed + jnp.einsum(
        "sh,dh->sd", grad_value, value_matrix, preferred_element_type=jnp.float32
    )
    grad_normed = lax.psum_scatter(
        summed.astype(jnp.bfloat16), "tp", scatter_dimension=0, tiled=True
    ).astype(jnp.float32)
    _, norm_one_back = jax.vjp(rms_norm, x_float, norm_gain)
    grad_x_norm, norm_gain_grad = norm_one_back(grad_normed)
    input_grad = grad_middle + grad_x_norm
    query_grad, key_grad, value_grad, out_grad = lax.psum(
        (query_grad, key_grad, value_grad, out_grad), "ep"
    )
    norm_gain_grad, moe_gain_grad, router_grad = lax.psum(
        (norm_gain_grad, moe_gain_grad, router_grad), ("ep", "tp")
    )
    return (
        output,
        input_grad,
        norm_gain_grad,
        query_grad,
        key_grad,
        value_grad,
        out_grad,
        moe_gain_grad,
        router_grad,
        gate_grad,
        up_grad,
        down_grad,
    )


def solution(mesh):
    in_specs = (
        P(("ep", "tp"), None),
        P(),
        P(None, "tp"),
        P(None, "tp"),
        P(None, "tp"),
        P("tp", None),
        P(),
        P(),
        P("ep", None, "tp"),
        P("ep", None, "tp"),
        P("ep", "tp", None),
        P(("ep", "tp"), None),
        P(("ep", "tp"), None),
        P("ep", None),
        P("ep", None),
    )
    out_specs = (
        P(("ep", "tp"), None),
        P(("ep", "tp"), None),
        P(),
        P(None, "tp"),
        P(None, "tp"),
        P(None, "tp"),
        P("tp", None),
        P(),
        P(),
        P("ep", None, "tp"),
        P("ep", None, "tp"),
        P("ep", "tp", None),
    )
    return jax.shard_map(local, mesh=mesh, in_specs=in_specs, out_specs=out_specs, check_vma=False)
```

profile of v0, /device:TPU:0, one launch (start us, length us, event | category | flops | bytes accessed | tf_op | source)
XLA Modules:
  0.0 2431.7 jit_solution(11049751359227529653)
XLA Ops:
  13.7 20.4 all-gather.7.cloned.1.call-done
  64.9 21.6 reduce-scatter.5.cloned.1.call-done
  104.7 100.1 %all-gather.13.cloned.1.call-done = bf16[4,8,160,1536]{3,2,1,0:T(8,128)(2,1)} async-done(((bf16[1,8,160,1536]{3,2,1,0:T(8,128)(2,1)}), bf16[4,8,160,1536]{3,2,1,0:T(8,128)(2,1)}) %all-gather.13.cloned.1.call-update) | async-done | bytes 15728656 | tf_op jit(solution)/shard_map/all_gather | solution.py:66
  231.7 100.5 %all-gather.9.cloned.1.call-done = bf16[4,8,160,1536]{3,2,1,0:T(8,128)(2,1)} async-done(((bf16[1,8,160,1536]{3,2,1,0:T(8,128)(2,1)}), bf16[4,8,160,1536]{3,2,1,0:T(8,128)(2,1)}) %all-gather.9.cloned.1.call-update) | async-done | bytes 15728656 | tf_op jit(solution)/shard_map/all_gather | solution.py:66
  332.1 13.2 copy.109
  345.4 219.3 %all-to-all-done.2 = bf16[4,8,160,1536]{3,2,0,1:T(8,128)(2,1)} async-done(((bf16[4,8,160,1536]{3,2,0,1:T(8,128)(2,1)}), bf16[4,8,160,1536]{3,2,0,1:T(8,128)(2,1)}, u32[]{:S(2)}, u32[]{:S(2)}) %all-to-all-start.2) | async-done | bytes 15728672 | tf_op jit(solution)/shard_map/all_to_all | solution.py:70
  582.5 328.5 %all-to-all-done = bf16[4,8,160,1536]{3,2,0,1:T(8,128)(2,1)} async-done(((bf16[4,8,160,1536]{3,2,0,1:T(8,128)(2,1)}), bf16[4,8,160,1536]{3,2,0,1:T(8,128)(2,1)}, u32[]{:S(2)}, u32[]{:S(2)}) %all-to-all-start) | async-done | bytes 15728672 | tf_op jit(solution)/shard_map/all_to_all | solution.py:70
  942.9 13.3 copy.113
  956.3 118.0 %reduce-scatter.7.cloned.1.call-done = bf16[1,8,160,1536]{3,2,1,0:T(8,128)(2,1)} async-done(((bf16[4,8,160,1536]{3,2,1,0:T(8,128)(2,1)}), bf16[1,8,160,1536]{3,2,1,0:T(8,128)(2,1)}) %reduce-scatter.7.cloned.1.call-update) | async-done | bytes 3932176 | tf_op jit(solution)/shard_map/reduce_scatter | solution.py:190
  1074.5 18.8 fusion.39
  1093.3 18.2 fusion.8
  1111.5 13.4 copy.118
  1125.0 50.9 %all-gather.11.cloned.1.call-done = bf16[4,8,160,1536]{3,2,1,0:T(8,128)(2,1)} async-done(((bf16[1,8,160,1536]{3,2,1,0:T(8,128)(2,1)}), bf16[4,8,160,1536]{3,2,1,0:T(8,128)(2,1)}) %all-gather.11.cloned.1.call-update) | async-done | bytes 15728656 | tf_op jit(solution)/shard_map/all_gather | solution.py:66
  1175.9 13.8 copy.114
  1195.9 102.7 %reduce-scatter.9.cloned.1.call-done = bf16[1,8,160,1536]{3,2,1,0:T(8,128)(2,1)} async-done(((bf16[4,8,160,1536]{3,2,1,0:T(8,128)(2,1)}), bf16[1,8,160,1536]{3,2,1,0:T(8,128)(2,1)}) %reduce-scatter.9.cloned.1.call-update) | async-done | bytes 3932176 | tf_op jit(solution)/shard_map/reduce_scatter | solution.py:246
  1298.6 101.6 %all-gather.15.cloned.1.call-done = bf16[4,8,160,1536]{3,2,1,0:T(8,128)(2,1)} async-done(((bf16[1,8,160,1536]{3,2,1,0:T(8,128)(2,1)}), bf16[4,8,160,1536]{3,2,1,0:T(8,128)(2,1)}) %all-gather.15.cloned.1.call-update) | async-done | bytes 15728656 | tf_op jit(solution)/shard_map/all_gather | solution.py:66
  1413.3 123.5 %all-to-all-done.1 = bf16[4,8,160,1536]{3,2,0,1:T(8,128)(2,1)} async-done(((bf16[4,8,160,1536]{3,2,0,1:T(8,128)(2,1)}), bf16[4,8,160,1536]{3,2,0,1:T(8,128)(2,1)}, u32[]{:S(2)}, u32[]{:S(2)}) %all-to-all-start.1) | async-done | bytes 15728672 | tf_op jit(solution)/shard_map/all_to_all | solution.py:74
  1542.8 340.0 %all-to-all-done.3 = bf16[4,8,160,1536]{3,2,0,1:T(8,128)(2,1)} async-done(((bf16[4,8,160,1536]{3,2,0,1:T(8,128)(2,1)}), bf16[4,8,160,1536]{3,2,0,1:T(8,128)(2,1)}, u32[]{:S(2)}, u32[]{:S(2)}) %all-to-all-start.3) | async-done | bytes 15728672 | tf_op jit(solution)/shard_map/all_to_all | solution.py:74
  1890.0 23.2 gather_fusion.1
  1913.2 23.2 gather_fusion
  1949.9 71.8 %all-gather.17.cloned.1.call-done = bf16[512,1536]{1,0:T(8,128)(2,1)} async-done(((bf16[128,1536]{1,0:T(8,128)(2,1)}), bf16[512,1536]{1,0:T(8,128)(2,1)}) %all-gather.17.cloned.1.call-update) | async-done | bytes 1572880 | tf_op jit(solution)/shard_map/all_gather | solution.py:264
  2084.5 39.3 %all-reduce.4 = (f32[1536]{0:T(1024)}, f32[1536]{0:T(1024)}) all-reduce(f32[1536]{0:T(1024)S(1)} %get-tuple-element.14, f32[1536]{0:T(1024)S(1)} %get-tuple-element.12), channel_id=1, replica_groups=mesh['ep'=8,'tp'=4] {'ep','tp'}, use_global_device_ids=true, to_apply=%region_23.24 | all-reduce | flops 3072 | bytes 24576 | tf_op jit(solution)/shard_map/psum | solution.py:323
  2126.2 71.5 %all-reduce.9.cloned.1.call-done = f32[1536,40]{0,1:T(8,128)} async-done(((f32[1536,40]{0,1:T(8,128)}), f32[1536,40]{0,1:T(8,128)}) %all-reduce.9.cloned.1.call-update) | async-done | bytes 245776 | tf_op jit(solution)/shard_map/psum | solution.py:323
  2197.7 219.5 %all-reduce.11.cloned.1.call-done = (f32[1536,384]{1,0:T(8,128)}, f32[1536,128]{1,0:T(8,128)}, f32[1536,128]{1,0:T(8,128)}, f32[384,1536]{1,0:T(8,128)}) async-done(((f32[1536,384]{1,0:T(8,128)}, f32[1536,128]{1,0:T(8,128)}, f32[1536,128]{1,0:T(8,128)}, f32[384,1536]{1,0:T(8,128)}), (f32[1536,384]{1,0:T(8,128)}, f32[1536,128]{1,0:T(8,128)}, f32[1536,128]{1,0:T(8,128)}, ...) | async-done | bytes 6291472 | tf_op jit(solution)/shard_map/psum | solution.py:320
  (320 shorter events, 249.3 us)
Async XLA Ops:
  7.2 915.5 %copy-start = (bf16[5,1536,128]{2,1,0:T(8,128)(2,1)S(1)}, bf16[5,1536,128]{2,1,0:T(8,128)(2,1)}, u32[]{:S(2)}) copy-start(bf16[5,1536,128]{2,1,0:T(8,128)(2,1)} %param.24) | copy-start | bytes 5898244
  7.2 26.9 %all-gather.7.cloned.1.call-start = ((), (), s32[]{:S(2)}) async-start(), calls=%async_computation.8 | async-start | bytes 1966080 | tf_op jit(solution)/shard_map/all_gather | solution.py:113
  11.6 75.0 %reduce-scatter.5.cloned.1.call-start = ((), (), s32[]{:S(2)}) async-start(), calls=%async_computation.9 | async-start | bytes 3932160 | tf_op jit(solution)/shard_map/reduce_scatter | solution.py:144
  48.4 156.5 %all-gather.13.cloned.1.call-start = ((), (), s32[]{:S(2)}) async-start(), calls=%async_computation.13 | async-start | bytes 19660800 | tf_op jit(solution)/shard_map/all_gather | solution.py:66
  88.1 135.6 %copy-start.14 = (bf16[128,1536]{1,0:T(8,128)(2,1)}, bf16[128,1536]{1,0:T(8,128)(2,1)S(1)}, u32[]{:S(2)}) copy-start(bf16[128,1536]{1,0:T(8,128)(2,1)S(1)} %multiply_convert_fusion) | copy-start | bytes 1179652
  218.0 346.7 %all-to-all-start.2 = ((bf16[4,8,160,1536]{3,2,0,1:T(8,128)(2,1)}), bf16[4,8,160,1536]{3,2,0,1:T(8,128)(2,1)}, u32[]{:S(2)}, u32[]{:S(2)}) async-start(bf16[4,8,160,1536]{3,2,0,1:T(8,128)(2,1)} %copy.115), calls=%async_computation.4 | async-start | bytes 31457280 | tf_op jit(solution)/shard_map/all_to_all | solution.py:70
  223.6 108.5 %all-gather.9.cloned.1.call-start = ((), (), s32[]{:S(2)}) async-start(), calls=%async_computation.10 | async-start | bytes 19660800 | tf_op jit(solution)/shard_map/all_gather | solution.py:66
  564.7 346.3 %all-to-all-start = ((bf16[4,8,160,1536]{3,2,0,1:T(8,128)(2,1)}), bf16[4,8,160,1536]{3,2,0,1:T(8,128)(2,1)}, u32[]{:S(2)}, u32[]{:S(2)}) async-start(bf16[4,8,160,1536]{3,2,0,1:T(8,128)(2,1)} %copy.109), calls=%async_computation.1 | async-start | bytes 31457280 | tf_op jit(solution)/shard_map/all_to_all | solution.py:70
  570.7 503.6 %reduce-scatter.7.cloned.1.call-start = ((), (), s32[]{:S(2)}) async-start(), calls=%async_computation.11 | async-start | bytes 19660800 | tf_op jit(solution)/shard_map/reduce_scatter | solution.py:190
  956.3 118.2 %copy-start.37 = (bf16[4,8,5,32,128]{4,3,1,0,2:T(8,128)(2,1)S(1)}, bf16[4,8,5,32,128]{4,3,1,0,2:T(8,128)(2,1)}, u32[]{:S(2)}) copy-start(bf16[4,8,5,32,128]{4,3,1,0,2:T(8,128)(2,1)} %get-tuple-element.29) | copy-start | bytes 3932164
  956.3 219.6 %all-gather.11.cloned.1.call-start = ((), (), s32[]{:S(2)}) async-start(), calls=%async_computation.12 | async-start | bytes 19660800 | tf_op jit(solution)/shard_map/all_gather | solution.py:66
  1074.4 224.1 %reduce-scatter.9.cloned.1.call-start = ((), (), s32[]{:S(2)}) async-start(), calls=%async_computation.14 | async-start | bytes 19660800 | tf_op jit(solution)/shard_map/reduce_scatter | solution.py:246
  1189.7 347.2 %all-to-all-start.1 = ((bf16[4,8,160,1536]{3,2,0,1:T(8,128)(2,1)}), bf16[4,8,160,1536]{3,2,0,1:T(8,128)(2,1)}, u32[]{:S(2)}, u32[]{:S(2)}) async-start(bf16[4,8,160,1536]{3,2,0,1:T(8,128)(2,1)} %copy.114), calls=%async_computation.3 | async-start | bytes 31457280 | tf_op jit(solution)/shard_map/all_to_all | solution.py:74
  1195.8 204.4 %all-gather.15.cloned.1.call-start = ((), (), s32[]{:S(2)}) async-start(), calls=%async_computation.15 | async-start | bytes 19660800 | tf_op jit(solution)/shard_map/all_gather | solution.py:66
  1413.3 129.4 %copy-start.76 = (f32[128]{0:T(128)S(1)}, f32[128]{0:T(128)}, u32[]{:S(2)}) copy-start(f32[128]{0:T(128)} %copy-done.75) | copy-start | bytes 1540
  1536.9 345.9 %all-to-all-start.3 = ((bf16[4,8,160,1536]{3,2,0,1:T(8,128)(2,1)}), bf16[4,8,160,1536]{3,2,0,1:T(8,128)(2,1)}, u32[]{:S(2)}, u32[]{:S(2)}) async-start(bf16[4,8,160,1536]{3,2,0,1:T(8,128)(2,1)} %copy.119), calls=%async_computation.6 | async-start | bytes 31457280 | tf_op jit(solution)/shard_map/all_to_all | solution.py:74
  1542.5 479.2 %all-gather.17.cloned.1.call-start = ((), (), s32[]{:S(2)}) async-start(), calls=%async_computation.16 | async-start | bytes 1966080 | tf_op jit(solution)/shard_map/all_gather | solution.py:264
  1542.8 347.2 %copy-start.2 = (s32[1024,1]{0,1:T(1,128)S(1)}, s32[1024,1]{0,1:T(1,128)}, u32[]{:S(2)}) copy-start(s32[1024,1]{0,1:T(1,128)} %get-tuple-element.41) | copy-start | bytes 12292
  1948.5 75.9 %copy-start.12 = (f32[128,1536]{1,0:T(8,128)}, f32[128,1536]{1,0:T(8,128)S(1)}, u32[]{:S(2)}) copy-start(f32[128,1536]{1,0:T(8,128)S(1)} %get-tuple-element.51) | copy-start | bytes 2359300
  1949.6 74.9 %copy-start.17 = (pred[512,512]{0,1:T(8,128)(4,1)S(1)}, pred[512,512]{0,1:T(8,128)(4,1)}, u32[]{:S(2)}) copy-start(pred[512,512]{0,1:T(8,128)(4,1)} %copy-done.16) | copy-start | bytes 786436
  1949.6 133.5 %reduce-scatter.11.cloned.1.call-start = ((), (), s32[]{:S(2)}) async-start(), calls=%async_computation.17 | async-start | bytes 1966080 | tf_op jit(solution)/shard_map/reduce_scatter | solution.py:314
  2039.5 158.2 %all-reduce.9.cloned.1.call-start = ((), (), s32[]{:S(2)}) async-start(), calls=%async_computation.18 | async-start | bytes 491520 | tf_op jit(solution)/shard_map/psum | solution.py:323
  2040.6 376.6 %all-reduce.11.cloned.1.call-start = ((), (), s32[]{:S(2)}) async-start(), calls=%async_computation.19 | async-start | bytes 12582912 | tf_op jit(solution)/shard_map/psum | solution.py:320
  2072.2 51.6 %copy-start.8 = (f32[128,1536]{1,0:T(8,128)S(1)}, f32[128,1536]{1,0:T(8,128)}, u32[]{:S(2)}) copy-start(f32[128,1536]{1,0:T(8,128)} %copy-done.6) | copy-start | bytes 2359300
  (83 other events, 816.1 us)
Sparse Core Ops, SparseCore 0:
  11.7 22.3 all-gather.6
  48.5 38.0 reduce-scatter.4
  104.8 99.9 all-gather.12
  231.8 100.3 all-gather.8
  956.4 117.9 reduce-scatter.6
  1075.9 99.9 all-gather.10
  1178.6 119.8 reduce-scatter.8
  1300.2 99.9 all-gather.14
  1949.7 71.9 all-gather.16
  2039.6 28.1 reduce-scatter.10
  2073.9 123.6 all-reduce.8
  2202.5 214.6 all-reduce.10
where the time goes:
time: 2440 us; the launch traced here: 2430 us
  waiting for transfers between devices  1990 us (82%)
  local copies, waits for them, and re-layouts  165 us (7%)
  matrix products  151 us (6%)
  other arithmetic  45.8 us (2%)
  blocking collectives  39.3 us (2%)
  starting transfers between devices  24.8 us (1%)
    all_to_all x2, waiting for transfers between devices, dispatch_rows(): return lax.all_to_all(boxes, 'ep', split_axis=1, concat_axis=1, tiled=True)  548 us
    all_to_all x2, waiting for transfers between devices, return_rows(): return lax.all_to_all(boxes, 'ep', split_axis=1, concat_axis=1, tiled=True)  464 us
    all_gather x4, waiting for transfers between devices, group_rows(): return lax.all_gather(boxes, 'tp', axis=0, tiled=True)  353 us
    psum x1, waiting for transfers between devices, local(): lax.psum((query_grad, key_grad, value_grad, out_grad), 'ep')  220 us
    reduce_scatter x1, waiting for transfers between devices, local(): lax.psum_scatter(result.reshape(1 * lax.axis_size('tp'), owners, local_ex...  118 us
    reduce_scatter x1, waiting for transfers between devices, local(): lax.psum_scatter(summed.reshape(1 * lax.axis_size('tp'), owners, local_ex...  103 us
    all_gather x1, waiting for transfers between devices, local(): lax.all_gather(grad_middle.astype(jnp.bfloat16), 'tp', axis=0, tiled=True)  71.8 us
    psum x1, waiting for transfers between devices, local(): lax.psum((norm_gain_grad, moe_gain_grad, router_grad), ('ep', 'tp'))  71.5 us
  transfers between devices with their start and end apart: 16, of which 15 were waited for; matrix products, arithmetic and copies ran while one was open for 7% of the time, Pallas kernels for 0%

commit v1 on v0

--- a/solution.py
+++ b/solution.py
@@ -1,3 +1,4 @@
+import functools
 import math
 import jax
 import jax.numpy as jnp
@@ -7,6 +8,15 @@
 HEAD_SIZE_DIM = 64
 EPS = 1e-06
 HIGH_PRECISION = lax.Precision.HIGHEST
+
+
+def name_loads_in(buf, mesh_name, a_name):
+    then = lax.psum(buf, axis_name=mesh_name)
+    w_next = lax.psum(then, axis_name=a_name)
+    return w_next
+
+
+process_plate = functools.partial(name_loads_in, mesh_name="tp", a_name="ep")
 
 
 def rms_norm(activation, gain_vec):
@@ -320,8 +330,8 @@
     query_grad, key_grad, value_grad, out_grad = lax.psum(
         (query_grad, key_grad, value_grad, out_grad), "ep"
     )
-    norm_gain_grad, moe_gain_grad, router_grad = lax.psum(
-        (norm_gain_grad, moe_gain_grad, router_grad), ("ep", "tp")
+    norm_gain_grad, moe_gain_grad, router_grad = process_plate(
+        (norm_gain_grad, moe_gain_grad, router_grad)
     )
     return (
         output,

time: 2440 us -> 2340 us (0.959)
  waiting for transfers between devices: 1990 us -> 1880 us
    psum x1, waiting for transfers between devices: 71.5 us -> 9.26 us  [name_loads_in(): then = lax.psum(buf, axis_name=mesh_name)]
    psum x1, waiting for transfers between devices: 220 us -> 174 us  [local(): lax.psum((query_grad, key_grad, value_grad, out_grad), 'ep')]
    psum x1 -> x2, blocking collectives: 39.3 us -> 50.4 us  [the longest x1 40.2 us: name_loads_in(): w_next = lax.psum(then, axis_name=a_name)]
  transfers between devices with their start and end apart: 16 -> 16, of which waited for: 15 -> 15; matrix products, arithmetic and copies ran while one was open for 7% -> 8% of each run, Pallas kernels for 0% -> 0%
where the time goes in v1:
time: 2340 us; the launch traced here: 2330 us
  waiting for transfers between devices  1880 us (80%)
  local copies, waits for them, and re-layouts  166 us (7%)
  matrix products  149 us (6%)
  blocking collectives  50.4 us (2%)
  other arithmetic  47.3 us (2%)
  starting transfers between devices  24.8 us (1%)
    all_to_all x2, waiting for transfers between devices, dispatch_rows(): return lax.all_to_all(boxes, 'ep', split_axis=1, concat_axis=1, tiled=True)  548 us
    all_to_all x2, waiting for transfers between devices, return_rows(): return lax.all_to_all(boxes, 'ep', split_axis=1, concat_axis=1, tiled=True)  464 us
    all_gather x4, waiting for transfers between devices, group_rows(): return lax.all_gather(boxes, 'tp', axis=0, tiled=True)  353 us
    psum x1, waiting for transfers between devices, local(): lax.psum((query_grad, key_grad, value_grad, out_grad), 'ep')  174 us
    reduce_scatter x1, waiting for transfers between devices, local(): lax.psum_scatter(result.reshape(1 * lax.axis_size('tp'), owners, local_ex...  118 us
    reduce_scatter x1, waiting for transfers between devices, local(): lax.psum_scatter(summed.reshape(1 * lax.axis_size('tp'), owners, local_ex...  103 us
    all_gather x1, waiting for transfers between devices, local(): lax.all_gather(grad_middle.astype(jnp.bfloat16), 'tp', axis=0, tiled=True)  69.3 us
    all_gather x4, local copies, waits for them, and re-layouts, group_rows(): return lax.all_gather(boxes, 'tp', axis=0, tiled=True)  53.3 us
  transfers between devices with their start and end apart: 16, of which 15 were waited for; matrix products, arithmetic and copies ran while one was open for 8% of the time, Pallas kernels for 0%

profile of v1, /device:TPU:0, one launch (start us, length us, event | category | flops | bytes accessed | tf_op | source)
XLA Modules:
  0.0 2333.2 jit_solution(10337978898196453238)
XLA Ops:
  13.7 20.4 all-gather.7.cloned.1.call-done
  65.0 21.6 reduce-scatter.5.cloned.1.call-done
  104.7 100.1 %all-gather.13.cloned.1.call-done = bf16[4,8,160,1536]{3,2,1,0:T(8,128)(2,1)} async-done(((bf16[1,8,160,1536]{3,2,1,0:T(8,128)(2,1)}), bf16[4,8,160,1536]{3,2,1,0:T(8,128)(2,1)}) %all-gather.13.cloned.1.call-update) | async-done | bytes 15728656 | tf_op jit(solution)/shard_map/all_gather | solution.py:76
  231.6 100.5 %all-gather.9.cloned.1.call-done = bf16[4,8,160,1536]{3,2,1,0:T(8,128)(2,1)} async-done(((bf16[1,8,160,1536]{3,2,1,0:T(8,128)(2,1)}), bf16[4,8,160,1536]{3,2,1,0:T(8,128)(2,1)}) %all-gather.9.cloned.1.call-update) | async-done | bytes 15728656 | tf_op jit(solution)/shard_map/all_gather | solution.py:76
  332.1 13.2 copy.109
  345.3 219.3 %all-to-all-done.2 = bf16[4,8,160,1536]{3,2,0,1:T(8,128)(2,1)} async-done(((bf16[4,8,160,1536]{3,2,0,1:T(8,128)(2,1)}), bf16[4,8,160,1536]{3,2,0,1:T(8,128)(2,1)}, u32[]{:S(2)}, u32[]{:S(2)}) %all-to-all-start.2) | async-done | bytes 15728672 | tf_op jit(solution)/shard_map/all_to_all | solution.py:80
  582.4 328.5 %all-to-all-done = bf16[4,8,160,1536]{3,2,0,1:T(8,128)(2,1)} async-done(((bf16[4,8,160,1536]{3,2,0,1:T(8,128)(2,1)}), bf16[4,8,160,1536]{3,2,0,1:T(8,128)(2,1)}, u32[]{:S(2)}, u32[]{:S(2)}) %all-to-all-start) | async-done | bytes 15728672 | tf_op jit(solution)/shard_map/all_to_all | solution.py:80
  942.8 13.3 copy.113
  956.2 118.0 %reduce-scatter.7.cloned.1.call-done = bf16[1,8,160,1536]{3,2,1,0:T(8,128)(2,1)} async-done(((bf16[4,8,160,1536]{3,2,1,0:T(8,128)(2,1)}), bf16[1,8,160,1536]{3,2,1,0:T(8,128)(2,1)}) %reduce-scatter.7.cloned.1.call-update) | async-done | bytes 3932176 | tf_op jit(solution)/shard_map/reduce_scatter | solution.py:200
  1074.3 18.8 fusion.39
  1093.1 18.3 fusion.8
  1111.4 13.4 copy.118
  1124.9 50.9 %all-gather.11.cloned.1.call-done = bf16[4,8,160,1536]{3,2,1,0:T(8,128)(2,1)} async-done(((bf16[1,8,160,1536]{3,2,1,0:T(8,128)(2,1)}), bf16[4,8,160,1536]{3,2,1,0:T(8,128)(2,1)}) %all-gather.11.cloned.1.call-update) | async-done | bytes 15728656 | tf_op jit(solution)/shard_map/all_gather | solution.py:76
  1175.7 13.8 copy.114
  1195.7 102.6 %reduce-scatter.9.cloned.1.call-done = bf16[1,8,160,1536]{3,2,1,0:T(8,128)(2,1)} async-done(((bf16[4,8,160,1536]{3,2,1,0:T(8,128)(2,1)}), bf16[1,8,160,1536]{3,2,1,0:T(8,128)(2,1)}) %reduce-scatter.9.cloned.1.call-update) | async-done | bytes 3932176 | tf_op jit(solution)/shard_map/reduce_scatter | solution.py:256
  1298.4 101.6 %all-gather.15.cloned.1.call-done = bf16[4,8,160,1536]{3,2,1,0:T(8,128)(2,1)} async-done(((bf16[1,8,160,1536]{3,2,1,0:T(8,128)(2,1)}), bf16[4,8,160,1536]{3,2,1,0:T(8,128)(2,1)}) %all-gather.15.cloned.1.call-update) | async-done | bytes 15728656 | tf_op jit(solution)/shard_map/all_gather | solution.py:76
  1400.0 13.2 copy.119
  1413.2 123.6 %all-to-all-done.1 = bf16[4,8,160,1536]{3,2,0,1:T(8,128)(2,1)} async-done(((bf16[4,8,160,1536]{3,2,0,1:T(8,128)(2,1)}), bf16[4,8,160,1536]{3,2,0,1:T(8,128)(2,1)}, u32[]{:S(2)}, u32[]{:S(2)}) %all-to-all-start.1) | async-done | bytes 15728672 | tf_op jit(solution)/shard_map/all_to_all | solution.py:84
  1542.6 340.0 %all-to-all-done.3 = bf16[4,8,160,1536]{3,2,0,1:T(8,128)(2,1)} async-done(((bf16[4,8,160,1536]{3,2,0,1:T(8,128)(2,1)}), bf16[4,8,160,1536]{3,2,0,1:T(8,128)(2,1)}, u32[]{:S(2)}, u32[]{:S(2)}) %all-to-all-start.3) | async-done | bytes 15728672 | tf_op jit(solution)/shard_map/all_to_all | solution.py:84
  1889.9 23.2 gather_fusion.1
  1913.1 23.2 gather_fusion
  1954.6 69.3 %all-gather.17.cloned.1.call-done = bf16[512,1536]{1,0:T(8,128)(2,1)} async-done(((bf16[128,1536]{1,0:T(8,128)(2,1)}), bf16[512,1536]{1,0:T(8,128)(2,1)}) %all-gather.17.cloned.1.call-update) | async-done | bytes 1572880 | tf_op jit(solution)/shard_map/all_gather | solution.py:274
  2102.4 40.2 %all-reduce.4 = (f32[1536]{0:T(1024)}, f32[1536]{0:T(1024)}) all-reduce(f32[1536]{0:T(1024)S(1)} %get-tuple-element.25, f32[1536]{0:T(1024)S(1)} %get-tuple-element.26), channel_id=1, replica_groups=mesh['ep'=8,'tp'=4] {'ep'}, use_global_device_ids=true, to_apply=%region_24.25 | all-reduce | flops 3072 | bytes 24576 | tf_op jit(solution)/shard_map/psum | solution.py:15
  2145.0 173.6 %all-reduce.12.cloned.1.call-done = (f32[1536,384]{1,0:T(8,128)}, f32[1536,128]{1,0:T(8,128)}, f32[1536,128]{1,0:T(8,128)}, f32[384,1536]{1,0:T(8,128)}, f32[1536,40]{0,1:T(8,128)}) async-done(((f32[1536,384]{1,0:T(8,128)}, f32[1536,128]{1,0:T(8,128)}, f32[1536,128]{1,0:T(8,128)}, f32[384,1536]{1,0:T(8,128)}, f32[1536,40]{0,1:T(8,128)}), (f32[1536,384]{1,0:T(8,128)}, f32[1536,128]{1,0:T(8,128)}, ...) | async-done | bytes 6537232 | tf_op jit(solution)/shard_map/psum | solution.py:330
  (327 shorter events, 256.7 us)
Async XLA Ops:
  7.2 915.5 %copy-start = (bf16[5,1536,128]{2,1,0:T(8,128)(2,1)S(1)}, bf16[5,1536,128]{2,1,0:T(8,128)(2,1)}, u32[]{:S(2)}) copy-start(bf16[5,1536,128]{2,1,0:T(8,128)(2,1)} %param.24) | copy-start | bytes 5898244
  7.2 26.9 %all-gather.7.cloned.1.call-start = ((), (), s32[]{:S(2)}) async-start(), calls=%async_computation.8 | async-start | bytes 1966080 | tf_op jit(solution)/shard_map/all_gather | solution.py:123
  11.6 74.9 %reduce-scatter.5.cloned.1.call-start = ((), (), s32[]{:S(2)}) async-start(), calls=%async_computation.9 | async-start | bytes 3932160 | tf_op jit(solution)/shard_map/reduce_scatter | solution.py:154
  48.4 156.4 %all-gather.13.cloned.1.call-start = ((), (), s32[]{:S(2)}) async-start(), calls=%async_computation.13 | async-start | bytes 19660800 | tf_op jit(solution)/shard_map/all_gather | solution.py:76
  88.1 135.5 %copy-start.14 = (bf16[128,1536]{1,0:T(8,128)(2,1)}, bf16[128,1536]{1,0:T(8,128)(2,1)S(1)}, u32[]{:S(2)}) copy-start(bf16[128,1536]{1,0:T(8,128)(2,1)S(1)} %multiply_convert_fusion) | copy-start | bytes 1179652
  217.9 346.7 %all-to-all-start.2 = ((bf16[4,8,160,1536]{3,2,0,1:T(8,128)(2,1)}), bf16[4,8,160,1536]{3,2,0,1:T(8,128)(2,1)}, u32[]{:S(2)}, u32[]{:S(2)}) async-start(bf16[4,8,160,1536]{3,2,0,1:T(8,128)(2,1)} %copy.115), calls=%async_computation.4 | async-start | bytes 31457280 | tf_op jit(solution)/shard_map/all_to_all | solution.py:80
  223.6 108.5 %all-gather.9.cloned.1.call-start = ((), (), s32[]{:S(2)}) async-start(), calls=%async_computation.10 | async-start | bytes 19660800 | tf_op jit(solution)/shard_map/all_gather | solution.py:76
  564.6 346.3 %all-to-all-start = ((bf16[4,8,160,1536]{3,2,0,1:T(8,128)(2,1)}), bf16[4,8,160,1536]{3,2,0,1:T(8,128)(2,1)}, u32[]{:S(2)}, u32[]{:S(2)}) async-start(bf16[4,8,160,1536]{3,2,0,1:T(8,128)(2,1)} %copy.109), calls=%async_computation.1 | async-start | bytes 31457280 | tf_op jit(solution)/shard_map/all_to_all | solution.py:80
  570.7 503.5 %reduce-scatter.7.cloned.1.call-start = ((), (), s32[]{:S(2)}) async-start(), calls=%async_computation.11 | async-start | bytes 19660800 | tf_op jit(solution)/shard_map/reduce_scatter | solution.py:200
  956.1 118.2 %copy-start.38 = (bf16[4,8,5,32,128]{4,3,1,0,2:T(8,128)(2,1)S(1)}, bf16[4,8,5,32,128]{4,3,1,0,2:T(8,128)(2,1)}, u32[]{:S(2)}) copy-start(bf16[4,8,5,32,128]{4,3,1,0,2:T(8,128)(2,1)} %get-tuple-element.32) | copy-start | bytes 3932164
  956.1 219.6 %all-gather.11.cloned.1.call-start = ((), (), s32[]{:S(2)}) async-start(), calls=%async_computation.12 | async-start | bytes 19660800 | tf_op jit(solution)/shard_map/all_gather | solution.py:76
  1074.2 224.1 %reduce-scatter.9.cloned.1.call-start = ((), (), s32[]{:S(2)}) async-start(), calls=%async_computation.14 | async-start | bytes 19660800 | tf_op jit(solution)/shard_map/reduce_scatter | solution.py:256
  1189.5 347.2 %all-to-all-start.1 = ((bf16[4,8,160,1536]{3,2,0,1:T(8,128)(2,1)}), bf16[4,8,160,1536]{3,2,0,1:T(8,128)(2,1)}, u32[]{:S(2)}, u32[]{:S(2)}) async-start(bf16[4,8,160,1536]{3,2,0,1:T(8,128)(2,1)} %copy.114), calls=%async_computation.3 | async-start | bytes 31457280 | tf_op jit(solution)/shard_map/all_to_all | solution.py:84
  1195.7 204.3 %all-gather.15.cloned.1.call-start = ((), (), s32[]{:S(2)}) async-start(), calls=%async_computation.15 | async-start | bytes 19660800 | tf_op jit(solution)/shard_map/all_gather | solution.py:76
  1413.2 129.4 %copy-start.77 = (f32[128]{0:T(128)S(1)}, f32[128]{0:T(128)}, u32[]{:S(2)}) copy-start(f32[128]{0:T(128)} %copy-done.76) | copy-start | bytes 1540
  1536.7 345.9 %all-to-all-start.3 = ((bf16[4,8,160,1536]{3,2,0,1:T(8,128)(2,1)}), bf16[4,8,160,1536]{3,2,0,1:T(8,128)(2,1)}, u32[]{:S(2)}, u32[]{:S(2)}) async-start(bf16[4,8,160,1536]{3,2,0,1:T(8,128)(2,1)} %copy.119), calls=%async_computation.6 | async-start | bytes 31457280 | tf_op jit(solution)/shard_map/all_to_all | solution.py:84
  1542.4 481.4 %all-gather.17.cloned.1.call-start = ((), (), s32[]{:S(2)}) async-start(), calls=%async_computation.16 | async-start | bytes 1966080 | tf_op jit(solution)/shard_map/all_gather | solution.py:274
  1542.6 347.2 %copy-start.2 = (s32[1024,1]{0,1:T(1,128)S(1)}, s32[1024,1]{0,1:T(1,128)}, u32[]{:S(2)}) copy-start(s32[1024,1]{0,1:T(1,128)} %get-tuple-element.44) | copy-start | bytes 12292
  1949.3 76.9 %copy-start.12 = (f32[128,1536]{1,0:T(8,128)}, f32[128,1536]{1,0:T(8,128)S(1)}, u32[]{:S(2)}) copy-start(f32[128,1536]{1,0:T(8,128)S(1)} %get-tuple-element.54) | copy-start | bytes 2359300
  1949.3 74.5 %copy-start.41 = (bf16[384,1536]{1,0:T(8,128)(2,1)S(1)}, bf16[384,1536]{1,0:T(8,128)(2,1)}, u32[]{:S(2)}) copy-start(bf16[384,1536]{1,0:T(8,128)(2,1)} %param.20) | copy-start | bytes 3538948
  1951.7 106.1 %all-reduce.10.cloned.1.call-start = ((), (), s32[]{:S(2)}) async-start(), calls=%async_computation.18 | async-start | bytes 491520 | tf_op jit(solution)/shard_map/psum | solution.py:14
  1954.3 71.9 %copy-start.17 = (pred[512,512]{0,1:T(8,128)(4,1)S(1)}, pred[512,512]{0,1:T(8,128)(4,1)}, u32[]{:S(2)}) copy-start(pred[512,512]{0,1:T(8,128)(4,1)} %copy-done.16) | copy-start | bytes 786436
  1954.3 136.5 %reduce-scatter.11.cloned.1.call-start = ((), (), s32[]{:S(2)}) async-start(), calls=%async_computation.17 | async-start | bytes 1966080 | tf_op jit(solution)/shard_map/reduce_scatter | solution.py:324
  2040.6 278.0 %all-reduce.12.cloned.1.call-start = ((), (), s32[]{:S(2)}) async-start(), calls=%async_computation.19 | async-start | bytes 13074432 | tf_op jit(solution)/shard_map/psum | solution.py:330
  (86 other events, 994.9 us)
Sparse Core Ops, SparseCore 0:
  11.7 22.3 all-gather.6
  48.5 37.9 reduce-scatter.4
  104.8 99.9 all-gather.12
  231.7 100.3 all-gather.8
  956.2 117.9 reduce-scatter.6
  1075.7 99.9 all-gather.10
  1178.5 119.8 reduce-scatter.8
  1300.0 99.9 all-gather.14
  1951.8 71.9 all-gather.16
  2026.7 31.0 all-reduce.9
  2060.3 28.8 reduce-scatter.10
  2095.2 223.3 all-reduce.11
